TPU v7x, 32 devices: a whole 2x2x4 slice. The times are simulated.
32 devices in a mesh: dp: 4 (over y, core), blk: 8 (over z, x).
Axes of the slice: x: 2, y: 2, z: 4, core: 2. Of those that a mesh axis runs over, the one named last changes fastest.
Arguments:
- q_raw: bfloat16 [4, 1024, 512], P('dp', 'blk'), may hold values from -8 to 8
- k_raw: bfloat16 [4, 1024, 128], P('dp', 'blk'), may hold values from -8 to 8
- values: bfloat16 [4, 1024, 128], P('dp', 'blk'), may hold values from -6 to 6
- out_grad: bfloat16 [4, 1024, 512], P('dp', 'blk'), may hold values from -60 to 60
- q_gain: float32 [128], replicated, may hold values from 0.5 to 5
- k_gain: float32 [128], replicated, may hold values from 0.5 to 5
- block_order: int32 [16], replicated, may hold values from 0 to 15, as said below
- seq_len: int32 [4], P('dp'), may hold values from 256 to 1024, as said below
Outputs:
- attended: bfloat16 [4, 1024, 512], P('dp', 'blk')
- q_grad: bfloat16 [4, 1024, 512], P('dp', 'blk')
- k_grad: bfloat16 [4, 1024, 128], P('dp', 'blk')
- v_grad: bfloat16 [4, 1024, 128], P('dp', 'blk')
- q_gain_grad: float32 [128], replicated
- k_gain_grad: float32 [128], replicated
Inputs may be any that keep to these rules, and one draw needn't show every extreme that they name: `block_order`: each number from 0 to 15 appears exactly once. `seq_len`: some sequence is full and some holds exactly 256 valid tokens.
All inputs are finite; a program needn't handle non-finite values.
Results may differ from a plain program's by a relative error of at most 0.02.
The roundings to bfloat16 on the way count: a program that leaves them out, or rounds other values in their place, can miss the bound.
Values may be sent and summed in bfloat16 or wider, within the bound.
A program may use at most 64 MiB of HBM per device.

v0:
```python
import jax
import jax.numpy as jnp
from jax import lax
from jax.sharding import PartitionSpec as P

EPSILON = 1e-06
NEG_FLOOR = -1e30


def norm_forward(raw_rows, gain_vec):
    inv_rms = lax.rsqrt(jnp.mean(raw_rows * raw_rows, axis=-1, keepdims=True) + EPSILON)
    return (raw_rows * inv_rms * gain_vec, inv_rms)


def norm_backward(raw_rows, inv_rms, gain_vec, grad_rows):
    scaled = gain_vec * grad_rows
    inner_mean = jnp.mean(raw_rows * scaled, axis=-1, keepdims=True)
    d_raw = inv_rms * scaled - raw_rows * inv_rms**3 * inner_mean
    d_gain = jnp.sum((grad_rows * raw_rows * inv_rms).reshape(-1, raw_rows.shape[-1]), axis=0)
    return (d_raw, d_gain)


def slot_positions(block_order, start_slot, slot_count, half_rows):
    slot_ids = start_slot + jnp.arange(slot_count, dtype=jnp.int32)
    block_ids = slot_ids // half_rows
    block_match = block_ids[:, None] == jnp.arange(block_order.shape[0], dtype=jnp.int32)[None, :]
    picked = jnp.sum(jnp.where(block_match, block_order[None, :], 0), axis=1)
    return picked * half_rows + slot_ids % half_rows


def allowed_mask(q_pos, k_pos, seq_length):
    return (k_pos[None, None, :] <= q_pos[:, None, None]) & (k_pos < seq_length)[None, None, :]


def forward_fold(softmax_state, key_rows, value_rows, k_pos, q_hat, q_pos, seq_length, score_scale):
    row_max, row_sum, mixed_sum = softmax_state
    scores = (
        jnp.einsum("thd,kd->thk", q_hat, key_rows, preferred_element_type=jnp.float32) * score_scale
    )
    scores = jnp.where(allowed_mask(q_pos, k_pos, seq_length), scores, -jnp.inf)
    new_max = jnp.maximum(row_max, jnp.max(scores, axis=-1))
    weights = jnp.exp(scores - new_max[..., None])
    row_sum = jnp.sum(weights, axis=-1)
    mixed_sum = jnp.einsum(
        "thk,kd->thd", weights.astype(jnp.bfloat16), value_rows, preferred_element_type=jnp.float32
    )
    return (new_max, row_sum, mixed_sum)


def grad_terms(
    q_hat,
    masked_grad,
    log_total,
    row_delta,
    q_pos,
    key_rows,
    value_rows,
    k_pos,
    seq_length,
    score_scale,
):
    scores = (
        jnp.einsum("thd,kd->thk", q_hat, key_rows, preferred_element_type=jnp.float32) * score_scale
    )
    scores = jnp.where(allowed_mask(q_pos, k_pos, seq_length), scores, -jnp.inf)
    prob_rows = jnp.exp(scores - log_total[..., None])
    dv_part = jnp.einsum(
        "thk,thd->kd",
        prob_rows.astype(jnp.bfloat16),
        masked_grad,
        preferred_element_type=jnp.float32,
    )
    prob_grad = jnp.einsum(
        "thd,kd->thk", masked_grad, value_rows, preferred_element_type=jnp.float32
    )
    score_grad = (prob_rows * (prob_grad - row_delta[..., None]) * score_scale).astype(jnp.bfloat16)
    dq_part = jnp.einsum("thk,kd->thd", score_grad, key_rows, preferred_element_type=jnp.float32)
    dk_part = jnp.einsum("thk,thd->kd", score_grad, q_hat, preferred_element_type=jnp.float32)
    return (dq_part, dk_part, dv_part)


def per_device(q_raw, k_raw, values, out_grad, q_gain, k_gain, block_order, seq_len):
    row_count = q_raw.shape[1]
    head_size = k_raw.shape[2]
    head_count = q_raw.shape[2] // head_size
    half_rows = row_count // 2
    score_scale = head_size ** (-0.5)
    seq_length = seq_len[0]
    first_slot = lax.axis_index("blk") * row_count
    q_pos = slot_positions(block_order, first_slot, row_count, half_rows)
    q_live = q_pos < seq_length
    q_float = q_raw[0].astype(jnp.float32).reshape(row_count, head_count, head_size)
    q_norm, q_inv = norm_forward(q_float, q_gain)
    q_hat = q_norm.astype(jnp.bfloat16)
    k_float = k_raw[0].astype(jnp.float32)
    k_norm, k_inv = norm_forward(k_float, k_gain)
    k_hat = k_norm.astype(jnp.bfloat16)
    own_values = values[0]
    own_grad = out_grad[0]
    masked_grad = jnp.where(q_live[:, None], own_grad, jnp.zeros_like(own_grad)).reshape(
        row_count, head_count, head_size
    )
    start_state = (
        jnp.full((row_count, head_count), NEG_FLOOR, jnp.float32),
        jnp.zeros((row_count, head_count), jnp.float32),
        jnp.zeros((row_count, head_count, head_size), jnp.float32),
    )
    key_rows = lax.all_gather(k_hat, "blk", axis=0, tiled=True)
    value_rows = lax.all_gather(own_values, "blk", axis=0, tiled=True)
    k_pos = slot_positions(block_order, jnp.int32(0), key_rows.shape[0], half_rows)
    softmax_state = forward_fold(
        start_state, key_rows, value_rows, k_pos, q_hat, q_pos, seq_length, score_scale
    )
    row_max, row_sum, mixed_sum = softmax_state
    out_rows = jnp.where(q_live[:, None, None], mixed_sum / row_sum[..., None], 0.0).astype(
        jnp.bfloat16
    )
    log_total = row_max + jnp.log(row_sum)
    row_delta = jnp.sum(masked_grad.astype(jnp.float32) * out_rows.astype(jnp.float32), axis=-1)
    key_rows = lax.all_gather(k_hat, "blk", axis=0, tiled=True)
    value_rows = lax.all_gather(own_values, "blk", axis=0, tiled=True)
    k_pos = slot_positions(block_order, jnp.int32(0), key_rows.shape[0], half_rows)
    dq_part, dk_part, dv_part = grad_terms(
        q_hat,
        masked_grad,
        log_total,
        row_delta,
        q_pos,
        key_rows,
        value_rows,
        k_pos,
        seq_length,
        score_scale,
    )
    dk_hat, dv_total = (
        lax.psum_scatter(
            dk_part.astype(jnp.bfloat16), "blk", scatter_dimension=0, tiled=True
        ).astype(jnp.float32),
        lax.psum_scatter(
            dv_part.astype(jnp.bfloat16), "blk", scatter_dimension=0, tiled=True
        ).astype(jnp.float32),
    )
    q_grad, q_gain_part = norm_backward(q_float, q_inv, q_gain, dq_part)
    k_grad, k_gain_part = norm_backward(k_float, k_inv, k_gain, dk_hat)
    q_gain_grad, k_gain_grad = lax.psum((q_gain_part, k_gain_part), ("dp", "blk"))
    return (
        out_rows.reshape(1, row_count, head_count * head_size),
        q_grad.astype(jnp.bfloat16).reshape(1, row_count, head_count * head_size),
        k_grad.astype(jnp.bfloat16)[None],
        dv_total.astype(jnp.bfloat16)[None],
        q_gain_grad,
        k_gain_grad,
    )


def solution(mesh):
    in_specs = (
        P("dp", "blk", None),
        P("dp", "blk", None),
        P("dp", "blk", None),
        P("dp", "blk", None),
        P(),
        P(),
        P(),
        P("dp"),
    )
    out_specs = (
        P("dp", "blk", None),
        P("dp", "blk", None),
        P("dp", "blk", None),
        P("dp", "blk", None),
        P(),
        P(),
    )
    return jax.shard_map(
        per_device, mesh=mesh, in_specs=in_specs, out_specs=out_specs, check_vma=False
    )
```

profile of v0, /device:TPU:0, one launch (start us, length us, event | category | flops | bytes accessed | tf_op | source)
XLA Modules:
  0.0 210.7 jit_solution(539508779636458118)
XLA Ops:
  7.2 1.0 copy.30
  8.9 0.9 fusion.19
  9.8 0.5 multiply_multiply_fusion.1
  10.4 0.8 fusion.21
  11.2 32.5 %all_gather.8 = bf16[1024,128]{1,0:T(8,128)(2,1)S(1)} all-gather(bf16[128,128]{1,0:T(8,128)(2,1)S(1)} %fusion.21), channel_id=1, replica_groups=mesh['dp'=4,'blk'=8] {'blk'}, dimensions={0}, use_global_device_ids=true | all-gather | bytes 294912 | tf_op jit(solution)/shard_map/all_gather | solution.py:108
  43.7 1.1 copy.27
  44.9 0.7 select_reduce_fusion.1
  45.6 0.7 select_reduce_fusion
  46.4 0.2 compare_and_fusion
  46.6 1.3 fusion.41
  48.0 26.4 %all-gather = bf16[1,1024,128]{1,2,0:T(8,128)(2,1)S(1)} all-gather(bf16[1,128,128]{1,2,0:T(8,128)(2,1)S(1)} %copy.29), channel_id=2, replica_groups=mesh['dp'=4,'blk'=8] {'blk'}, dimensions={1}, use_global_device_ids=true | all-gather | bytes 294912 | tf_op jit(solution)/shard_map/all_gather | solution.py:109
  74.5 0.5 fusion
  75.0 1.3 multiply_reduce_fusion.2
  76.2 1.3 multiply_convert_fusion
  77.5 1.2 fusion.3
  78.8 2.0 fusion.4
  80.9 1.6 multiply_reduce_fusion
  82.5 0.8 copy.38
  83.4 0.8 copy.39
  84.2 55.4 %reduce-scatter.3.cloned.1.call-done = bf16[128,128]{1,0:T(8,128)(2,1)} async-done(((bf16[1024,128]{1,0:T(8,128)(2,1)}), bf16[128,128]{1,0:T(8,128)(2,1)}) %reduce-scatter.3.cloned.1.call-update) | async-done | bytes 32784 | tf_op jit(solution)/shard_map/reduce_scatter | solution.py:136
  139.6 0.9 fusion.25
  140.5 40.2 %all-reduce = (f32[128]{0:T(128)}, f32[128]{0:T(128)}) all-reduce(f32[128]{0:T(128)S(1)} %get-tuple-element.18, f32[128]{0:T(128)S(1)} %get-tuple-element.20), channel_id=1, replica_groups=mesh['dp'=4,'blk'=8] {'dp','blk'}, use_global_device_ids=true, to_apply=%region_12.13 | all-reduce | flops 256 | bytes 2048 | tf_op jit(solution)/shard_map/psum | solution.py:145
  180.7 1.5 fusion.28
  182.2 21.7 %reduce-scatter.5.cloned.1.call-done = bf16[128,128]{1,0:T(8,128)(2,1)} async-done(((bf16[1024,128]{1,0:T(8,128)(2,1)}), bf16[128,128]{1,0:T(8,128)(2,1)}) %reduce-scatter.5.cloned.1.call-update) | async-done | bytes 32784 | tf_op jit(solution)/shard_map/reduce_scatter | solution.py:139
  (37 shorter events, 0.5 us)
Async XLA Ops:
  7.2 132.4 %reduce-scatter.3.cloned.1.call-start = ((), (), s32[]{:S(2)}) async-start(), calls=%async_computation.2 | async-start | bytes 294912 | tf_op jit(solution)/shard_map/reduce_scatter | solution.py:136
  7.2 40.7 %copy-start.3 = (bf16[1,128,128]{2,1,0:T(8,128)(2,1)S(1)}, bf16[1,128,128]{2,1,0:T(8,128)(2,1)}, u32[]{:S(2)}) copy-start(bf16[1,128,128]{2,1,0:T(8,128)(2,1)} %param.10) | copy-start | bytes 98308
  10.3 37.6 %copy-start.6 = (f32[128]{0:T(128)}, f32[128]{0:T(128)S(1)}, u32[]{:S(2)}) copy-start(f32[128]{0:T(128)S(1)} %get-tuple-element.29) | copy-start | bytes 1540
  43.7 31.2 %copy-start = (bf16[1024,128]{1,0:T(8,128)(2,1)}, bf16[1024,128]{1,0:T(8,128)(2,1)S(1)}, u32[]{:S(2)}) copy-start(bf16[1024,128]{1,0:T(8,128)(2,1)S(1)} %all_gather.8) | copy-start | bytes 786436
  46.4 29.8 %copy-start.8 = (pred[128]{0:T(512)(128)(4,1)}, pred[128]{0:T(512)(128)(4,1)S(1)}, u32[]{:S(2)}) copy-start(pred[128]{0:T(512)(128)(4,1)S(1)} %get-tuple-element.24) | copy-start | bytes 388
  76.2 1.3 copy-start.4
  78.8 125.0 %reduce-scatter.5.cloned.1.call-start = ((), (), s32[]{:S(2)}) async-start(), calls=%async_computation.3 | async-start | bytes 294912 | tf_op jit(solution)/shard_map/reduce_scatter | solution.py:139
  80.8 1.7 copy-start.2
  80.8 58.7 %copy-start.1 = (bf16[1,128,128]{2,1,0:T(8,128)(2,1)S(1)}, bf16[1,128,128]{2,1,0:T(8,128)(2,1)}, u32[]{:S(2)}) copy-start(bf16[1,128,128]{2,1,0:T(8,128)(2,1)} %param.9) | copy-start | bytes 98308
  80.9 58.7 %copy-start.5 = (f32[128]{0:T(128)S(1)}, f32[128]{0:T(128)}, u32[]{:S(2)}) copy-start(f32[128]{0:T(128)} %param.13) | copy-start | bytes 1540
  80.9 58.7 %copy-start.7 = (f32[128]{0:T(128)S(1)}, f32[128]{0:T(128)}, u32[]{:S(2)}) copy-start(f32[128]{0:T(128)} %copy-done.6) | copy-start | bytes 1540
  80.9 99.8 %copy-start.9 = (f32[128]{0:T(128)S(1)}, f32[128]{0:T(128)}, u32[]{:S(2)}) copy-start(f32[128]{0:T(128)} %get-tuple-element.28) | copy-start | bytes 1540
Sparse Core Ops, SparseCore 0:
  78.9 60.6 reduce-scatter.2
  143.5 60.3 reduce-scatter.4
where the time goes:
time: 211 us
  blocking collectives  99.1 us (47%)
  waiting for transfers between devices  77.1 us (37%)
  between operations  14.9 us (7%)
  matrix products  8.69 us (4%)
  other arithmetic  6.95 us (3%)
  local copies, waits for them, and re-layouts  3.82 us (2%)
    reduce_scatter x1, waiting for transfers between devices, per_device(): lax.psum_scatter(dk_part.astype(jnp.bfloat16), 'blk', scatter_dimension=0...  55.4 us
    psum x1, blocking collectives, per_device(): lax.psum((q_gain_part, k_gain_part), ('dp', 'blk'))  40.2 us
    all_gather x1, blocking collectives, per_device(): key_rows = lax.all_gather(k_hat, 'blk', axis=0, tiled=True)  32.5 us
    all_gather x1, blocking collectives, per_device(): value_rows = lax.all_gather(own_values, 'blk', axis=0, tiled=True)  26.4 us
    reduce_scatter x1, waiting for transfers between devices, per_device(): lax.psum_scatter(dv_part.astype(jnp.bfloat16), 'blk', scatter_dimension=0...  21.7 us
  transfers between devices with their start and end apart: 2, of which 2 were waited for; matrix products, arithmetic and copies ran while one was open for 4% of the time, Pallas kernels for 0%

commit v1 on v0

v1 whole, which is shorter than its diff:
```python
import functools

import jax
import jax.numpy as jnp
from jax import lax
from jax.experimental import pallas as pl
from jax.experimental.pallas import tpu as pltpu
from jax.sharding import PartitionSpec as P

EPSILON = 1e-06
MASKED = -1e30
FAR = 1 << 30
LOG2E = 1.4426950408889634
F32 = jnp.float32
BF16 = jnp.bfloat16


def loop(low, high, body, carry):
    if high - low <= 8:
        for i in range(low, high):
            carry = body(i, carry)
        return carry
    return lax.fori_loop(low, high, body, carry)


def dot_nt(a, b):
    return lax.dot_general(a, b, (((1,), (1,)), ((), ())), preferred_element_type=F32)


def dot_nn(a, b):
    return lax.dot_general(a, b, (((1,), (0,)), ((), ())), preferred_element_type=F32)


def dot_tn(a, b):
    return lax.dot_general(a, b, (((0,), (0,)), ((), ())), preferred_element_type=F32)


def kernel(
    n, groups, order_ref, len_ref, q_ref, k_ref, v_ref, go_ref, qg_ref, kg_ref,
    att_ref, qgrad_ref, kgrad_ref, vgrad_ref, qgain_ref, kgain_ref,
    kv, score, pgrad, dsend, drecv, gain1, gain2, q_hats, g_rows,
    kv_send, kv_recv, d_send, d_recv, g1_send, g1_recv, g2_send, g2_recv,
):
    rows, hd = k_ref.shape
    heads = q_ref.shape[1] // hd
    half = rows // 2
    me = lax.axis_index("blk")
    group = lax.axis_index("dp")
    scale = hd ** (-0.5)

    barrier = pltpu.get_barrier_semaphore()

    def greet(i, _):
        pl.semaphore_signal(barrier, inc=1, device_id={"blk": lax.rem(me + i, n)}, device_id_type=pl.DeviceIdType.MESH)
        return _

    def greet_group(i, _):
        pl.semaphore_signal(barrier, inc=1, device_id={"dp": lax.rem(group + i, groups)}, device_id_type=pl.DeviceIdType.MESH)
        return _

    loop(1, n, greet, 0)
    loop(1, groups, greet_group, 0)

    def kv_copy(i):
        return pltpu.make_async_remote_copy(
            src_ref=kv.at[0], dst_ref=kv.at[i], send_sem=kv_send.at[i], recv_sem=kv_recv.at[i],
            device_id={"blk": lax.rem(me + i, n)}, device_id_type=pl.DeviceIdType.MESH)

    def d_copy(i):
        return pltpu.make_async_remote_copy(
            src_ref=dsend.at[i], dst_ref=drecv.at[i], send_sem=d_send.at[i], recv_sem=d_recv.at[i],
            device_id={"blk": lax.rem(me - i + n, n)}, device_id_type=pl.DeviceIdType.MESH)

    def g1_copy(i, slot):
        return pltpu.make_async_remote_copy(
            src_ref=gain1.at[slot], dst_ref=gain1.at[slot], send_sem=g1_send.at[i], recv_sem=g1_recv.at[i],
            device_id={"blk": lax.rem(me + i, n)}, device_id_type=pl.DeviceIdType.MESH)

    def g2_copy(i, slot):
        return pltpu.make_async_remote_copy(
            src_ref=gain2.at[slot], dst_ref=gain2.at[slot], send_sem=g2_send.at[i], recv_sem=g2_recv.at[i],
            device_id={"dp": lax.rem(group + i, groups)}, device_id_type=pl.DeviceIdType.MESH)

    k_gain = kg_ref[...]
    q_gain = qg_ref[...]
    k_float = k_ref[...].astype(F32)
    k_inv = lax.rsqrt(jnp.mean(k_float * k_float, axis=-1, keepdims=True) + EPSILON)
    kv[0, :, :hd] = (k_float * k_inv * k_gain).astype(BF16)
    kv[0, :, hd:] = v_ref[...]

    pl.semaphore_wait(barrier, n - 1 + groups - 1)

    def start_kv(i, _):
        kv_copy(i).start()
        return _

    loop(1, n, start_kv, 0)

    seq_length = len_ref[0]

    def positions(owner, axis, shape):
        ids = lax.broadcasted_iota(jnp.int32, shape, axis)
        first = order_ref[2 * owner] * half
        second = order_ref[2 * owner + 1] * half - half
        return ids + jnp.where(ids < half, first, second)

    q_pos = jnp.concatenate([positions(me, 1, (1, rows))] * heads, axis=1)
    live_lane = q_pos < seq_length
    live_rows = positions(me, 0, (rows, hd)) < seq_length
    q_invs = []
    g_cols = []
    for h in range(heads):
        cut = slice(h * hd, (h + 1) * hd)
        q_float = q_ref[:, cut].astype(F32)
        q_inv = lax.rsqrt(jnp.mean(q_float * q_float, axis=-1, keepdims=True) + EPSILON)
        q_invs.append(q_inv)
        q_hats[h * rows:(h + 1) * rows, :] = (q_float * q_inv * q_gain).astype(BF16)
        g_float = jnp.where(live_rows, go_ref[:, cut].astype(F32), 0.0)
        g_rows[h * rows:(h + 1) * rows, :] = g_float.astype(BF16)
        g_cols.append(jnp.transpose(g_float))
    g_cols = jnp.concatenate(g_cols, axis=1)

    def first_pass(i, top):
        k_pos = positions(lax.rem(me - i + n, n), 0, (rows, heads * rows))
        k_pos = jnp.where(k_pos < seq_length, k_pos, FAR)
        s = dot_nt(kv[i, :, :hd], q_hats[...]) * (scale * LOG2E)
        s = jnp.where(k_pos <= q_pos, s, MASKED)
        score[i] = s
        pgrad[i] = dot_nt(kv[i, :, hd:], g_rows[...])
        return jnp.maximum(top, jnp.max(s, axis=0, keepdims=True))

    def first_pass_remote(i, top):
        kv_copy(i).wait_recv()
        return first_pass(i, top)

    top = first_pass(0, jnp.full((1, heads * rows), MASKED, F32))
    top = loop(1, n, first_pass_remote, top)

    def second_pass(i, carry):
        total, mixed = carry
        w = jnp.exp2(score[i] - top)
        score[i] = w
        total = total + jnp.sum(w, axis=0, keepdims=True)
        mixed = mixed + dot_tn(kv[i, :, hd:], w.astype(BF16))
        return total, mixed

    total, mixed = loop(
        0, n, second_pass,
        (jnp.zeros((1, heads * rows), F32), jnp.zeros((hd, heads * rows), F32)))
    inverse = 1.0 / total
    attended = jnp.where(live_lane, mixed * inverse, 0.0).astype(BF16).astype(F32)
    delta = jnp.sum(attended * g_cols, axis=0, keepdims=True)

    def third_pass(i, dq):
        p = score[i] * inverse
        ds = (p * (pgrad[i] - delta) * scale).astype(BF16)
        dk = dot_nn(ds, q_hats[...])
        dv = dot_nn(p.astype(BF16), g_rows[...])
        dq = dq + dot_tn(kv[i, :, :hd], ds)
        return dq, dk, dv

    def third_pass_remote(i, dq):
        dq, dk, dv = third_pass(i, dq)
        dsend[i, :, :hd] = dk.astype(BF16)
        dsend[i, :, hd:] = dv.astype(BF16)
        d_copy(i).start()
        return dq

    dq = loop(1, n, third_pass_remote, jnp.zeros((hd, heads * rows), F32))
    dq, dk, dv = third_pass(0, dq)

    part_q = jnp.zeros((1, hd), F32)
    part_k = jnp.zeros((1, hd), F32)
    dq_rows = []
    for h in range(heads):
        cut = slice(h * hd, (h + 1) * hd)
        dq_h = jnp.transpose(dq[:, h * rows:(h + 1) * rows])
        dq_rows.append(dq_h)
        q_float = q_ref[:, cut].astype(F32)
        part_q = part_q + jnp.sum(dq_h * q_float * q_invs[h], axis=0, keepdims=True)
        q_hat = q_hats[h * rows:(h + 1) * rows, :].astype(F32)
        part_k = part_k + jnp.sum(dq_h * q_hat, axis=0, keepdims=True)
    gain1[me, 0:1, :] = part_q
    gain1[me, 1:2, :] = part_k / k_gain

    def start_g1(i, _):
        g1_copy(i, me).start()
        return _

    loop(1, n, start_g1, 0)

    for h in range(heads):
        cut = slice(h * hd, (h + 1) * hd)
        q_float = q_ref[:, cut].astype(F32)
        q_inv = q_invs[h]
        scaled = q_gain * dq_rows[h]
        inner = jnp.mean(q_float * scaled, axis=-1, keepdims=True)
        qgrad_ref[:, cut] = (q_inv * scaled - q_float * (q_inv * q_inv * q_inv * inner)).astype(BF16)
        att_ref[:, cut] = jnp.transpose(attended[:, h * rows:(h + 1) * rows]).astype(BF16)

    def wait_g1(i, _):
        g1_copy(i, lax.rem(me - i + n, n)).wait_recv()
        return _

    loop(1, n, wait_g1, 0)
    gain2[group] = loop(1, n, lambda i, acc: acc + gain1[i], gain1[0])

    def start_g2(i, _):
        g2_copy(i, group).start()
        return _

    loop(1, groups, start_g2, 0)

    def gather(i, carry):
        dk, dv = carry
        d_copy(i).wait_recv()
        return dk + drecv[i, :, :hd].astype(F32), dv + drecv[i, :, hd:].astype(F32)

    dk, dv = loop(1, n, gather, (dk, dv))
    vgrad_ref[...] = dv.astype(BF16)
    scaled = k_gain * dk
    inner = jnp.mean(k_float * scaled, axis=-1, keepdims=True)
    kgrad_ref[...] = (k_inv * scaled - k_float * (k_inv * k_inv * k_inv * inner)).astype(BF16)

    def wait_g2(i, _):
        g2_copy(i, lax.rem(group - i + groups, groups)).wait_recv()
        return _

    loop(1, groups, wait_g2, 0)
    gains = loop(1, groups, lambda i, acc: acc + gain2[i], gain2[0])
    qgain_ref[...] = gains[0:1, :]
    kgain_ref[...] = gains[1:2, :]

    def drain(i, _):
        kv_copy(i).wait_send()
        d_copy(i).wait_send()
        g1_copy(i, me).wait_send()
        return _

    loop(1, n, drain, 0)

    def drain_group(i, _):
        g2_copy(i, group).wait_send()
        return _

    loop(1, groups, drain_group, 0)


def per_device(n, groups, q_raw, k_raw, values, out_grad, q_gain, k_gain, block_order, seq_len):
    rows, wide = q_raw.shape[1:]
    hd = k_raw.shape[2]
    lanes = (wide // hd) * rows
    vmem = pl.BlockSpec(memory_space=pltpu.VMEM)
    smem = pl.BlockSpec(memory_space=pltpu.SMEM)
    dma = pltpu.SemaphoreType.DMA
    out = pl.pallas_call(
        functools.partial(kernel, n, groups),
        out_shape=[
            jax.ShapeDtypeStruct((rows, wide), BF16),
            jax.ShapeDtypeStruct((rows, wide), BF16),
            jax.ShapeDtypeStruct((rows, hd), BF16),
            jax.ShapeDtypeStruct((rows, hd), BF16),
            jax.ShapeDtypeStruct((1, hd), F32),
            jax.ShapeDtypeStruct((1, hd), F32),
        ],
        in_specs=[smem, smem] + [vmem] * 6,
        out_specs=[vmem] * 6,
        scratch_shapes=[
            pltpu.VMEM((n, rows, 2 * hd), BF16),
            pltpu.VMEM((n, rows, lanes), F32),
            pltpu.VMEM((n, rows, lanes), F32),
            pltpu.VMEM((n, rows, 2 * hd), BF16),
            pltpu.VMEM((n, rows, 2 * hd), BF16),
            pltpu.VMEM((n, 2, hd), F32),
            pltpu.VMEM((groups, 2, hd), F32),
            pltpu.VMEM((lanes, hd), BF16),
            pltpu.VMEM((lanes, hd), BF16),
            dma((n,)), dma((n,)), dma((n,)), dma((n,)),
            dma((n,)), dma((n,)), dma((groups,)), dma((groups,)),
        ],
        compiler_params=pltpu.CompilerParams(
            collective_id=0, has_side_effects=True,
            vmem_limit_bytes=(16 + n) * 2**20),
    )(
        block_order, seq_len, q_raw[0], k_raw[0], values[0], out_grad[0],
        q_gain[None], k_gain[None],
    )
    attended, q_grad, k_grad, v_grad, q_gain_grad, k_gain_grad = out
    return (attended[None], q_grad[None], k_grad[None], v_grad[None], q_gain_grad[0], k_gain_grad[0])


def solution(mesh):
    tokens = P("dp", "blk", None)
    in_specs = (tokens, tokens, tokens, tokens, P(), P(), P(), P("dp"))
    out_specs = (tokens, tokens, tokens, tokens, P(), P())
    return jax.shard_map(
        functools.partial(per_device, mesh.shape["blk"], mesh.shape["dp"]),
        mesh=mesh, in_specs=in_specs, out_specs=out_specs, check_vma=False)
```

time: 211 us -> 47 us (0.22)
  blocking collectives: 99.1 us -> 0 us
  waiting for transfers between devices: 77.1 us -> 0 us
  Pallas kernels: 0 us -> 37.8 us
  between operations: 14.9 us -> 1.32 us
  matrix products: 8.69 us -> 0 us
  other arithmetic: 6.95 us -> 0 us
  local copies, waits for them, and re-layouts: 3.82 us -> 7.55 us
    reduce_scatter x2 -> x0, waiting for transfers between devices: 77.1 us -> none  [the longest x1 55.4 us: per_device(): lax.psum_scatter(dk_part.astype(jnp.bfloat16), 'blk', scatter_dimension=0...]
    all_gather x2 -> x0, blocking collectives: 59 us -> none  [the longest x1 32.5 us: per_device(): key_rows = lax.all_gather(k_hat, 'blk', axis=0, tiled=True)]
    psum x1 -> x0, blocking collectives: 40.2 us -> none  [per_device(): lax.psum((q_gain_part, k_gain_part), ('dp', 'blk'))]
    pallas_call x0 -> x1, Pallas kernels: none -> 37.8 us  [per_device(): pl.pallas_call(functools.partial(kernel, n, groups), out_shape=[jax.Shape...]
    dot_general x6 -> x0, matrix products: 8.69 us -> none  [the longest x1 2.01 us: grad_terms(): jnp.einsum('thk,thd->kd', prob_rows.astype(jnp.bfloat16), masked_grad, pr...]
    unnamed x24 -> x20, local copies, waits for them, and re-layouts: 2.72 us -> 7.55 us
    reduce_sum x6 -> x0, other arithmetic: 3.75 us -> none  [the longest x2 1.48 us: slot_positions(): picked = jnp.sum(jnp.where(block_match, block_order[None, :], 0), axis=1)]
  transfers between devices with their start and end apart: 2 -> 0, of which waited for: 2 -> 0; matrix products, arithmetic and copies ran while one was open for 4% -> 0% of each run, Pallas kernels for 0% -> 0%
where the time goes in v1:
time: 47 us; the launch traced here: 46.7 us
  Pallas kernels  37.8 us (80%)
  local copies, waits for them, and re-layouts  7.55 us (16%)
  between operations  1.32 us (3%)
    pallas_call x1, Pallas kernels, per_device(): pl.pallas_call(functools.partial(kernel, n, groups), out_shape=[jax.Shape...  37.8 us
    unnamed x20, local copies, waits for them, and re-layouts  7.55 us

profile of v1, /device:TPU:0, one launch (start us, length us, event | category | flops | bytes accessed | tf_op | source)
XLA Modules:
  0.0 46.7 jit_solution(9864287606364827012)
XLA Ops:
  1.3 0.0 copy-start.4
  1.3 0.0 copy-start.5
  1.3 0.0 copy-start.6
  1.3 0.6 %copy-done.4 = s32[16]{0:T(128)S(1)} copy-done((s32[16]{0:T(128)S(1)}, s32[16]{0:T(128)}, u32[]{:S(2)}) %copy-start.4) | copy-done | bytes 88
  1.9 0.0 copy-done.5
  2.0 0.0 copy-done.6
  2.0 0.0 copy-start
  2.0 0.9 %copy-done = bf16[1,128,512]{2,1,0:T(8,128)(2,1)S(1)} copy-done((bf16[1,128,512]{2,1,0:T(8,128)(2,1)S(1)}, bf16[1,128,512]{2,1,0:T(8,128)(2,1)}, u32[]{:S(2)}) %copy-start) | copy-done | bytes 131096
  2.9 0.0 copy-start.1
  2.9 0.9 %copy-done.1 = bf16[1,128,512]{2,1,0:T(8,128)(2,1)S(1)} copy-done((bf16[1,128,512]{2,1,0:T(8,128)(2,1)S(1)}, bf16[1,128,512]{2,1,0:T(8,128)(2,1)}, u32[]{:S(2)}) %copy-start.1) | copy-done | bytes 131096
  3.8 0.0 copy-start.2
  3.8 0.8 %copy-done.2 = bf16[1,128,128]{2,1,0:T(8,128)(2,1)S(1)} copy-done((bf16[1,128,128]{2,1,0:T(8,128)(2,1)S(1)}, bf16[1,128,128]{2,1,0:T(8,128)(2,1)}, u32[]{:S(2)}) %copy-start.2) | copy-done | bytes 32792
  4.5 0.0 copy-start.3
  4.5 0.8 %copy-done.3 = bf16[1,128,128]{2,1,0:T(8,128)(2,1)S(1)} copy-done((bf16[1,128,128]{2,1,0:T(8,128)(2,1)S(1)}, bf16[1,128,128]{2,1,0:T(8,128)(2,1)}, u32[]{:S(2)}) %copy-start.3) | copy-done | bytes 32792
  5.3 37.8 %shard_map.127 = (bf16[128,512]{1,0:T(8,128)(2,1)S(1)}, bf16[128,512]{1,0:T(8,128)(2,1)S(1)}, bf16[128,128]{1,0:T(8,128)(2,1)S(1)}, bf16[128,128]{1,0:T(8,128)(2...) custom-call(s32[16]{0:T(128)S(1)} %copy-done.4, s32[1]{0:T(128)S(6)} %copy.20.len_ref, ...), custom_call_target="tpu_custom_call" | custom-call | tf_op jit(solution)/shard_map/pallas_call | solution.py:256
  43.1 0.7 %copy.21 = bf16[1,128,512]{2,1,0:T(8,128)(2,1)} copy(bf16[1,128,512]{2,1,0:T(8,128)(2,1)S(1)} %bitcast.15) | data formatting | bytes 262144
  43.8 0.7 %copy.22 = bf16[1,128,512]{2,1,0:T(8,128)(2,1)} copy(bf16[1,128,512]{2,1,0:T(8,128)(2,1)S(1)} %bitcast.14) | data formatting | bytes 262144
  44.4 0.6 %copy.23 = bf16[1,128,128]{2,1,0:T(8,128)(2,1)} copy(bf16[1,128,128]{2,1,0:T(8,128)(2,1)S(1)} %bitcast.19) | data formatting | bytes 65536
  45.0 0.6 %copy.24 = bf16[1,128,128]{2,1,0:T(8,128)(2,1)} copy(bf16[1,128,128]{2,1,0:T(8,128)(2,1)S(1)} %bitcast.18) | data formatting | bytes 65536
  45.6 0.5 %copy.25 = f32[128]{0:T(128)} copy(f32[128]{0:T(128)S(1)} %bitcast.23) | data formatting | bytes 1024
  46.1 0.5 %copy.26 = f32[128]{0:T(128)} copy(f32[128]{0:T(128)S(1)} %bitcast.22) | data formatting | bytes 1024
Async XLA Ops:
  1.3 0.7 %copy-start.4 = (s32[16]{0:T(128)S(1)}, s32[16]{0:T(128)}, u32[]{:S(2)}) copy-start(s32[16]{0:T(128)} %order_ref.1) | copy-start | bytes 196
  1.3 0.7 %copy-start.5 = (f32[128]{0:T(128)S(1)}, f32[128]{0:T(128)}, u32[]{:S(2)}) copy-start(f32[128]{0:T(128)} %param.12) | copy-start | bytes 1540
  1.3 0.7 %copy-start.6 = (f32[128]{0:T(128)S(1)}, f32[128]{0:T(128)}, u32[]{:S(2)}) copy-start(f32[128]{0:T(128)} %param.13) | copy-start | bytes 1540
  2.0 0.9 %copy-start = (bf16[1,128,512]{2,1,0:T(8,128)(2,1)S(1)}, bf16[1,128,512]{2,1,0:T(8,128)(2,1)}, u32[]{:S(2)}) copy-start(bf16[1,128,512]{2,1,0:T(8,128)(2,1)} %param.8) | copy-start | bytes 393220
  2.9 0.9 %copy-start.1 = (bf16[1,128,512]{2,1,0:T(8,128)(2,1)S(1)}, bf16[1,128,512]{2,1,0:T(8,128)(2,1)}, u32[]{:S(2)}) copy-start(bf16[1,128,512]{2,1,0:T(8,128)(2,1)} %param.11) | copy-start | bytes 393220
  3.8 0.8 %copy-start.2 = (bf16[1,128,128]{2,1,0:T(8,128)(2,1)S(1)}, bf16[1,128,128]{2,1,0:T(8,128)(2,1)}, u32[]{:S(2)}) copy-start(bf16[1,128,128]{2,1,0:T(8,128)(2,1)} %param.9) | copy-start | bytes 98308
  4.5 0.8 %copy-start.3 = (bf16[1,128,128]{2,1,0:T(8,128)(2,1)S(1)}, bf16[1,128,128]{2,1,0:T(8,128)(2,1)}, u32[]{:S(2)}) copy-start(bf16[1,128,128]{2,1,0:T(8,128)(2,1)} %param.10) | copy-start | bytes 98308

commit v2 on v1

--- a/solution.py
+++ b/solution.py
@@ -36,10 +36,12 @@
 
 
 def kernel(
-    n, groups, order_ref, len_ref, q_ref, k_ref, v_ref, go_ref, qg_ref, kg_ref,
-    att_ref, qgrad_ref, kgrad_ref, vgrad_ref, qgain_ref, kgain_ref,
-    kv, score, pgrad, dsend, drecv, gain1, gain2, q_hats, g_rows,
-    kv_send, kv_recv, d_send, d_recv, g1_send, g1_recv, g2_send, g2_recv,
+    n, groups, order_ref, len_ref, q_hbm, k_hbm, v_hbm, go_hbm, qg_hbm, kg_hbm,
+    att_hbm, qgrad_hbm, kgrad_hbm, vgrad_hbm, qgain_hbm, kgain_hbm,
+    q_ref, k_ref, go_ref, qg_ref, kg_ref, in_sem,
+    att_ref, qgrad_ref, kgrad_ref, vgrad_ref, qgain_ref, kgain_ref, out_sem,
+    kv, score, pgrad, xsend, xrecv, zsend, zrecv, gain1, gain2, q_hats, g_rows,
+    kv_send, kv_recv, x_send, x_recv, z_send, z_recv, g1_send, g1_recv, g2_send, g2_recv,
 ):
     rows, hd = k_ref.shape
     heads = q_ref.shape[1] // hd
@@ -47,6 +49,25 @@
     me = lax.axis_index("blk")
     group = lax.axis_index("dp")
     scale = hd ** (-0.5)
+    lines = n // 2
+    line, side = me // 2, lax.rem(me, 2)
+    partner = 2 * line + 1 - side
+
+    def owner_of(slot):
+        other = lax.rem(side + slot % 2, 2)
+        return 2 * lax.rem(line - slot // 2 + lines, lines) + other
+
+    loads = [
+        pltpu.make_async_copy(src, dst, in_sem.at[i]) for i, (src, dst) in enumerate([
+            (k_hbm, k_ref), (kg_hbm, kg_ref), (v_hbm, kv.at[0, :, pl.ds(hd, hd)]),
+            (q_hbm, q_ref), (qg_hbm, qg_ref), (go_hbm, go_ref)])]
+    for load in loads:
+        load.start()
+
+    stores = [
+        pltpu.make_async_copy(src, dst, out_sem.at[i]) for i, (src, dst) in enumerate([
+            (att_ref, att_hbm), (qgrad_ref, qgrad_hbm), (vgrad_ref, vgrad_hbm),
+            (kgrad_ref, kgrad_hbm), (qgain_ref, qgain_hbm), (kgain_ref, kgain_hbm)])]
 
     barrier = pltpu.get_barrier_semaphore()
 
@@ -61,15 +82,24 @@
     loop(1, n, greet, 0)
     loop(1, groups, greet_group, 0)
 
-    def kv_copy(i):
+    def push(src, dst, send, recv, i, device):
         return pltpu.make_async_remote_copy(
-            src_ref=kv.at[0], dst_ref=kv.at[i], send_sem=kv_send.at[i], recv_sem=kv_recv.at[i],
-            device_id={"blk": lax.rem(me + i, n)}, device_id_type=pl.DeviceIdType.MESH)
-
-    def d_copy(i):
-        return pltpu.make_async_remote_copy(
-            src_ref=dsend.at[i], dst_ref=drecv.at[i], send_sem=d_send.at[i], recv_sem=d_recv.at[i],
-            device_id={"blk": lax.rem(me - i + n, n)}, device_id_type=pl.DeviceIdType.MESH)
+            src_ref=src, dst_ref=dst, send_sem=send.at[i], recv_sem=recv.at[i],
+            device_id={"blk": device}, device_id_type=pl.DeviceIdType.MESH)
+
+    def kv_line(j):
+        device = 2 * lax.rem(line + j, lines) + side
+        return push(kv.at[0], kv.at[2 * j], kv_send, kv_recv, 2 * j, device)
+
+    def kv_side(j):
+        return push(kv.at[2 * j], kv.at[2 * j + 1], kv_send, kv_recv, 2 * j + 1, partner)
+
+    def d_side(j):
+        return push(xsend.at[j], xrecv.at[j], x_send, x_recv, j, partner)
+
+    def d_line(j):
+        device = 2 * lax.rem(line - j + lines, lines) + side
+        return push(zsend.at[j], zrecv.at[j], z_send, z_recv, j, device)
 
     def g1_copy(i, slot):
         return pltpu.make_async_remote_copy(
@@ -81,20 +111,25 @@
             src_ref=gain2.at[slot], dst_ref=gain2.at[slot], send_sem=g2_send.at[i], recv_sem=g2_recv.at[i],
             device_id={"dp": lax.rem(group + i, groups)}, device_id_type=pl.DeviceIdType.MESH)
 
+    for load in loads[:3]:
+        load.wait()
     k_gain = kg_ref[...]
-    q_gain = qg_ref[...]
     k_float = k_ref[...].astype(F32)
     k_inv = lax.rsqrt(jnp.mean(k_float * k_float, axis=-1, keepdims=True) + EPSILON)
     kv[0, :, :hd] = (k_float * k_inv * k_gain).astype(BF16)
-    kv[0, :, hd:] = v_ref[...]
 
     pl.semaphore_wait(barrier, n - 1 + groups - 1)
 
-    def start_kv(i, _):
-        kv_copy(i).start()
-        return _
-
-    loop(1, n, start_kv, 0)
+    kv_side(0).start()
+
+    def start_kv(j, _):
+        kv_line(j).start()
+        return _
+
+    loop(1, lines, start_kv, 0)
+    for load in loads[3:]:
+        load.wait()
+    q_gain = qg_ref[...]
 
     seq_length = len_ref[0]
 
@@ -121,7 +156,7 @@
     g_cols = jnp.concatenate(g_cols, axis=1)
 
     def first_pass(i, top):
-        k_pos = positions(lax.rem(me - i + n, n), 0, (rows, heads * rows))
+        k_pos = positions(owner_of(i), 0, (rows, heads * rows))
         k_pos = jnp.where(k_pos < seq_length, k_pos, FAR)
         s = dot_nt(kv[i, :, :hd], q_hats[...]) * (scale * LOG2E)
         s = jnp.where(k_pos <= q_pos, s, MASKED)
@@ -129,12 +164,17 @@
         pgrad[i] = dot_nt(kv[i, :, hd:], g_rows[...])
         return jnp.maximum(top, jnp.max(s, axis=0, keepdims=True))
 
-    def first_pass_remote(i, top):
-        kv_copy(i).wait_recv()
-        return first_pass(i, top)
+    def first_pass_remote(j, top):
+        kv_line(j).wait_recv()
+        kv_side(j).start()
+        top = first_pass(2 * j, top)
+        kv_side(j - 1).wait_recv()
+        return first_pass(2 * j - 1, top)
 
     top = first_pass(0, jnp.full((1, heads * rows), MASKED, F32))
-    top = loop(1, n, first_pass_remote, top)
+    top = loop(1, lines, first_pass_remote, top)
+    kv_side(lines - 1).wait_recv()
+    top = first_pass(n - 1, top)
 
     def second_pass(i, carry):
         total, mixed = carry
@@ -159,14 +199,24 @@
         dq = dq + dot_tn(kv[i, :, :hd], ds)
         return dq, dk, dv
 
-    def third_pass_remote(i, dq):
-        dq, dk, dv = third_pass(i, dq)
-        dsend[i, :, :hd] = dk.astype(BF16)
-        dsend[i, :, hd:] = dv.astype(BF16)
-        d_copy(i).start()
+    def other_side(step, dq):
+        j = (step + 1) % lines
+        dq, dk, dv = third_pass(2 * j + 1, dq)
+        xsend[j, :, :hd] = dk.astype(BF16)
+        xsend[j, :, hd:] = dv.astype(BF16)
+        d_side(j).start()
         return dq
 
-    dq = loop(1, n, third_pass_remote, jnp.zeros((hd, heads * rows), F32))
+    def own_side(j, dq):
+        dq, dk, dv = third_pass(2 * j, dq)
+        d_side(j).wait_recv()
+        zsend[j, :, :hd] = (dk + xrecv[j, :, :hd].astype(F32)).astype(BF16)
+        zsend[j, :, hd:] = (dv + xrecv[j, :, hd:].astype(F32)).astype(BF16)
+        d_line(j).start()
+        return dq
+
+    dq = loop(0, lines, other_side, jnp.zeros((hd, heads * rows), F32))
+    dq = loop(1, lines, own_side, dq)
     dq, dk, dv = third_pass(0, dq)
 
     part_q = jnp.zeros((1, hd), F32)
@@ -198,6 +248,9 @@
         qgrad_ref[:, cut] = (q_inv * scaled - q_float * (q_inv * q_inv * q_inv * inner)).astype(BF16)
         att_ref[:, cut] = jnp.transpose(attended[:, h * rows:(h + 1) * rows]).astype(BF16)
 
+    stores[0].start()
+    stores[1].start()
+
     def wait_g1(i, _):
         g1_copy(i, lax.rem(me - i + n, n)).wait_recv()
         return _
@@ -211,16 +264,23 @@
 
     loop(1, groups, start_g2, 0)
 
-    def gather(i, carry):
+    d_side(0).wait_recv()
+    dk = dk + xrecv[0, :, :hd].astype(F32)
+    dv = dv + xrecv[0, :, hd:].astype(F32)
+
+    def gather(j, carry):
         dk, dv = carry
-        d_copy(i).wait_recv()
-        return dk + drecv[i, :, :hd].astype(F32), dv + drecv[i, :, hd:].astype(F32)
-
-    dk, dv = loop(1, n, gather, (dk, dv))
+        d_line(j).wait_recv()
+        return dk + zrecv[j, :, :hd].astype(F32), dv + zrecv[j, :, hd:].astype(F32)
+
+    dk, dv = loop(1, lines, gather, (dk, dv))
     vgrad_ref[...] = dv.astype(BF16)
+    stores[2].start()
     scaled = k_gain * dk
     inner = jnp.mean(k_float * scaled, axis=-1, keepdims=True)
     kgrad_ref[...] = (k_inv * scaled - k_float * (k_inv * k_inv * k_inv * inner)).astype(BF16)
+
+    stores[3].start()
 
     def wait_g2(i, _):
         g2_copy(i, lax.rem(group - i + groups, groups)).wait_recv()
@@ -230,27 +290,52 @@
     gains = loop(1, groups, lambda i, acc: acc + gain2[i], gain2[0])
     qgain_ref[...] = gains[0:1, :]
     kgain_ref[...] = gains[1:2, :]
+    stores[4].start()
+    stores[5].start()
 
     def drain(i, _):
-        kv_copy(i).wait_send()
-        d_copy(i).wait_send()
         g1_copy(i, me).wait_send()
         return _
 
     loop(1, n, drain, 0)
+
+    def drain_side(j, _):
+        kv_side(j).wait_send()
+        d_side(j).wait_send()
+        return _
+
+    def drain_line(j, _):
+        kv_line(j).wait_send()
+        d_line(j).wait_send()
+        return _
+
+    loop(0, lines, drain_side, 0)
+    loop(1, lines, drain_line, 0)
 
     def drain_group(i, _):
         g2_copy(i, group).wait_send()
         return _
 
     loop(1, groups, drain_group, 0)
+    for store in stores:
+        store.wait()
+
+
+def store_kernel(*refs):
+    count = len(refs) // 2
+    sems = refs[2 * count]
+    copies = [pltpu.make_async_copy(refs[i], refs[count + i], sems.at[i]) for i in range(count)]
+    for copy in copies:
+        copy.start()
+    for copy in copies:
+        copy.wait()
 
 
 def per_device(n, groups, q_raw, k_raw, values, out_grad, q_gain, k_gain, block_order, seq_len):
     rows, wide = q_raw.shape[1:]
     hd = k_raw.shape[2]
     lanes = (wide // hd) * rows
-    vmem = pl.BlockSpec(memory_space=pltpu.VMEM)
+    hbm = pl.BlockSpec(memory_space=pltpu.HBM)
     smem = pl.BlockSpec(memory_space=pltpu.SMEM)
     dma = pltpu.SemaphoreType.DMA
     out = pl.pallas_call(
@@ -263,28 +348,52 @@
             jax.ShapeDtypeStruct((1, hd), F32),
             jax.ShapeDtypeStruct((1, hd), F32),
         ],
-        in_specs=[smem, smem] + [vmem] * 6,
-        out_specs=[vmem] * 6,
+        in_specs=[smem, smem] + [hbm] * 6,
+        out_specs=[hbm] * 6,
         scratch_shapes=[
+            pltpu.VMEM((rows, wide), BF16),
+            pltpu.VMEM((rows, hd), BF16),
+            pltpu.VMEM((rows, wide), BF16),
+            pltpu.VMEM((1, hd), F32),
+            pltpu.VMEM((1, hd), F32),
+            dma((6,)),
+            pltpu.VMEM((rows, wide), BF16),
+            pltpu.VMEM((rows, wide), BF16),
+            pltpu.VMEM((rows, hd), BF16),
+            pltpu.VMEM((rows, hd), BF16),
+            pltpu.VMEM((1, hd), F32),
+            pltpu.VMEM((1, hd), F32),
+            dma((6,)),
             pltpu.VMEM((n, rows, 2 * hd), BF16),
             pltpu.VMEM((n, rows, lanes), F32),
             pltpu.VMEM((n, rows, lanes), F32),
-            pltpu.VMEM((n, rows, 2 * hd), BF16),
-            pltpu.VMEM((n, rows, 2 * hd), BF16),
+            pltpu.VMEM((n // 2, rows, 2 * hd), BF16),
+            pltpu.VMEM((n // 2, rows, 2 * hd), BF16),
+            pltpu.VMEM((n // 2, rows, 2 * hd), BF16),
+            pltpu.VMEM((n // 2, rows, 2 * hd), BF16),
             pltpu.VMEM((n, 2, hd), F32),
             pltpu.VMEM((groups, 2, hd), F32),
             pltpu.VMEM((lanes, hd), BF16),
             pltpu.VMEM((lanes, hd), BF16),
-            dma((n,)), dma((n,)), dma((n,)), dma((n,)),
+            dma((n,)), dma((n,)),
+            dma((n // 2,)), dma((n // 2,)), dma((n // 2,)), dma((n // 2,)),
             dma((n,)), dma((n,)), dma((groups,)), dma((groups,)),
         ],
         compiler_params=pltpu.CompilerParams(
             collective_id=0, has_side_effects=True,
-            vmem_limit_bytes=(16 + n) * 2**20),
+            vmem_limit_bytes=60 * 2**20),
     )(
         block_order, seq_len, q_raw[0], k_raw[0], values[0], out_grad[0],
         q_gain[None], k_gain[None],
     )
+    out = pl.pallas_call(
+        store_kernel,
+        out_shape=[jax.ShapeDtypeStruct(o.shape, o.dtype) for o in out],
+        in_specs=[hbm] * len(out),
+        out_specs=[hbm] * len(out),
+        scratch_shapes=[dma((len(out),))],
+        compiler_params=pltpu.CompilerParams(vmem_limit_bytes=60 * 2**20),
+    )(*out)
     attended, q_grad, k_grad, v_grad, q_gain_grad, k_gain_grad = out
     return (attended[None], q_grad[None], k_grad[None], v_grad[None], q_gain_grad[0], k_gain_grad[0])
 

time: 47 us -> 45.8 us (0.974)
  local copies, waits for them, and re-layouts: 7.55 us -> 0 us
  Pallas kernels: 37.8 us -> 44.4 us
    pallas_call x0 -> x1, Pallas kernels: none -> 11.1 us  [per_device(): pl.pallas_call(store_kernel, out_shape=[jax.ShapeDtypeStruct(o.shape, o.d...]
    unnamed x20 -> x0, local copies, waits for them, and re-layouts: 7.55 us -> none
    pallas_call x1, Pallas kernels: 37.8 us -> 33.2 us  [per_device(): pl.pallas_call(functools.partial(kernel, n, groups), out_shape=[jax.Shape...]
where the time goes in v2:
time: 45.8 us; the launch traced here: 45.6 us
  Pallas kernels  44.4 us (97%)
  between operations  1.29 us (3%)
    pallas_call x1, Pallas kernels, per_device(): pl.pallas_call(functools.partial(kernel, n, groups), out_shape=[jax.Shape...  33.2 us
    pallas_call x1, Pallas kernels, per_device(): pl.pallas_call(store_kernel, out_shape=[jax.ShapeDtypeStruct(o.shape, o.d...  11.1 us

profile of v2, /device:TPU:0, one launch (start us, length us, event | category | flops | bytes accessed | tf_op | source)
XLA Modules:
  0.0 45.6 jit_solution(8371923427896797591)
XLA Ops:
  1.3 33.2 %shard_map.127 = (bf16[128,512]{1,0:T(8,128)(2,1)}, bf16[128,512]{1,0:T(8,128)(2,1)}, bf16[128,128]{1,0:T(8,128)(2,1)}, bf16[128,128]{1,0:T(8,128)(2,1)}, f32[1,128]{1,0:T(1,128)}, /*index=5*/f32[1,128]{1,0:T(1,128)}) custom-call(s32[16]{0:T(128)} %order_ref.1, s32[1]{0:T(128)S(6)} %copy.14.len_ref, bf16[128,512]{1,0:T(8,128)(2,1)} %bitcast.12, ...), custom_call_target="tpu_custom_call" | custom-call | tf_op jit(solution)/shard_map/pallas_call | solution.py:341
  34.5 11.1 %shard_map.128 = (bf16[128,512]{1,0:T(8,128)(2,1)}, bf16[128,512]{1,0:T(8,128)(2,1)}, bf16[128,128]{1,0:T(8,128)(2,1)}, bf16[128,128]{1,0:T(8,128)(2,1)}, f32[1,128]{1,0:T(1,128)}, /*index=5*/f32[1,128]{1,0:T(1,128)}) custom-call(bf16[128,512]{1,0:T(8,128)(2,1)} %get-tuple-element.18.refs_0_, bf16[128,512]{1,0:T(8,128)(2,1)} %get-tuple-element.19.refs_1_, ...), custom_call_target="tpu_custom_call" | custom-call | tf_op jit(solution)/shard_map/pallas_call | solution.py:389

commit v3 on v2

--- a/solution.py
+++ b/solution.py
@@ -322,13 +322,18 @@
 
 
 def store_kernel(*refs):
-    count = len(refs) // 2
-    sems = refs[2 * count]
-    copies = [pltpu.make_async_copy(refs[i], refs[count + i], sems.at[i]) for i in range(count)]
-    for copy in copies:
-        copy.start()
-    for copy in copies:
-        copy.wait()
+    count = (len(refs) - 2) // 3
+    sources, targets, held = refs[:count], refs[count:2 * count], refs[2 * count:3 * count]
+    in_sem, out_sem = refs[3 * count:]
+    loads = [pltpu.make_async_copy(sources[i], held[i], in_sem.at[i]) for i in range(count)]
+    stores = [pltpu.make_async_copy(held[i], targets[i], out_sem.at[i]) for i in range(count)]
+    for load in loads:
+        load.start()
+    for load, store in zip(loads, stores):
+        load.wait()
+        store.start()
+    for store in stores:
+        store.wait()
 
 
 def per_device(n, groups, q_raw, k_raw, values, out_grad, q_gain, k_gain, block_order, seq_len):
@@ -391,7 +396,7 @@
         out_shape=[jax.ShapeDtypeStruct(o.shape, o.dtype) for o in out],
         in_specs=[hbm] * len(out),
         out_specs=[hbm] * len(out),
-        scratch_shapes=[dma((len(out),))],
+        scratch_shapes=[pltpu.VMEM(o.shape, o.dtype) for o in out] + [dma((len(out),)), dma((len(out),))],
         compiler_params=pltpu.CompilerParams(vmem_limit_bytes=60 * 2**20),
     )(*out)
     attended, q_grad, k_grad, v_grad, q_gain_grad, k_gain_grad = out

time: 45.8 us -> 36.4 us (0.79)
  Pallas kernels: 44.4 us -> 35 us
    pallas_call x1, Pallas kernels: 11.1 us -> 1.75 us  [per_device(): pl.pallas_call(store_kernel, out_shape=[jax.ShapeDtypeStruct(o.shape, o.d...]
where the time goes in v3:
time: 36.4 us; the launch traced here: 36.3 us
  Pallas kernels  35 us (96%)
  between operations  1.29 us (4%)
    pallas_call x1, Pallas kernels, per_device(): pl.pallas_call(functools.partial(kernel, n, groups), out_shape=[jax.Shape...  33.2 us
    pallas_call x1, Pallas kernels, per_device(): pl.pallas_call(store_kernel, out_shape=[jax.ShapeDtypeStruct(o.shape, o.d...  1.75 us

profile of v3, /device:TPU:0, one launch (start us, length us, event | category | flops | bytes accessed | tf_op | source)
XLA Modules:
  0.0 36.3 jit_solution(7722331391045807219)
XLA Ops:
  1.3 33.2 %shard_map.127 = (bf16[128,512]{1,0:T(8,128)(2,1)}, bf16[128,512]{1,0:T(8,128)(2,1)}, bf16[128,128]{1,0:T(8,128)(2,1)}, bf16[128,128]{1,0:T(8,128)(2,1)}, f32[1,128]{1,0:T(1,128)}, /*index=5*/f32[1,128]{1,0:T(1,128)}) custom-call(s32[16]{0:T(128)} %order_ref.1, s32[1]{0:T(128)S(6)} %copy.14.len_ref, bf16[128,512]{1,0:T(8,128)(2,1)} %bitcast.12, ...), custom_call_target="tpu_custom_call" | custom-call | tf_op jit(solution)/shard_map/pallas_call | solution.py:346
  34.5 1.7 %shard_map.128 = (bf16[128,512]{1,0:T(8,128)(2,1)}, bf16[128,512]{1,0:T(8,128)(2,1)}, bf16[128,128]{1,0:T(8,128)(2,1)}, bf16[128,128]{1,0:T(8,128)(2,1)}, f32[1,128]{1,0:T(1,128)}, /*index=5*/f32[1,128]{1,0:T(1,128)}) custom-call(bf16[128,512]{1,0:T(8,128)(2,1)} %get-tuple-element.18.refs_0_, bf16[128,512]{1,0:T(8,128)(2,1)} %get-tuple-element.19.refs_1_, ...), custom_call_target="tpu_custom_call" | custom-call | tf_op jit(solution)/shard_map/pallas_call | solution.py:394

commit v4 on v3

--- a/solution.py
+++ b/solution.py
@@ -54,8 +54,8 @@
     partner = 2 * line + 1 - side
 
     def owner_of(slot):
-        other = lax.rem(side + slot % 2, 2)
-        return 2 * lax.rem(line - slot // 2 + lines, lines) + other
+        other = lax.rem(side + slot // lines, 2)
+        return 2 * lax.rem(line - slot % lines + lines, lines) + other
 
     loads = [
         pltpu.make_async_copy(src, dst, in_sem.at[i]) for i, (src, dst) in enumerate([
@@ -89,10 +89,10 @@
 
     def kv_line(j):
         device = 2 * lax.rem(line + j, lines) + side
-        return push(kv.at[0], kv.at[2 * j], kv_send, kv_recv, 2 * j, device)
+        return push(kv.at[0], kv.at[j], kv_send, kv_recv, j, device)
 
     def kv_side(j):
-        return push(kv.at[2 * j], kv.at[2 * j + 1], kv_send, kv_recv, 2 * j + 1, partner)
+        return push(kv.at[j], kv.at[lines + j], kv_send, kv_recv, lines + j, partner)
 
     def d_side(j):
         return push(xsend.at[j], xrecv.at[j], x_send, x_recv, j, partner)
@@ -156,10 +156,11 @@
     g_cols = jnp.concatenate(g_cols, axis=1)
 
     def first_pass(i, top):
-        k_pos = positions(owner_of(i), 0, (rows, heads * rows))
+        k_pos = positions(owner_of(i), 0, (rows, rows))
         k_pos = jnp.where(k_pos < seq_length, k_pos, FAR)
+        bias = jnp.where(k_pos <= q_pos[:, :rows], 0.0, MASKED)
         s = dot_nt(kv[i, :, :hd], q_hats[...]) * (scale * LOG2E)
-        s = jnp.where(k_pos <= q_pos, s, MASKED)
+        s = s + jnp.concatenate([bias] * heads, axis=1)
         score[i] = s
         pgrad[i] = dot_nt(kv[i, :, hd:], g_rows[...])
         return jnp.maximum(top, jnp.max(s, axis=0, keepdims=True))
@@ -167,57 +168,70 @@
     def first_pass_remote(j, top):
         kv_line(j).wait_recv()
         kv_side(j).start()
-        top = first_pass(2 * j, top)
+        top = first_pass(j, top)
         kv_side(j - 1).wait_recv()
-        return first_pass(2 * j - 1, top)
+        return first_pass(lines + j - 1, top)
 
     top = first_pass(0, jnp.full((1, heads * rows), MASKED, F32))
     top = loop(1, lines, first_pass_remote, top)
     kv_side(lines - 1).wait_recv()
     top = first_pass(n - 1, top)
 
-    def second_pass(i, carry):
+    def second_pass(p, carry):
         total, mixed = carry
-        w = jnp.exp2(score[i] - top)
-        score[i] = w
+        pair = pl.ds(2 * p, 2)
+        w = jnp.exp2(score[pair].reshape(2 * rows, heads * rows) - top)
+        score[pair] = w.reshape(2, rows, heads * rows)
         total = total + jnp.sum(w, axis=0, keepdims=True)
-        mixed = mixed + dot_tn(kv[i, :, hd:], w.astype(BF16))
+        mixed = mixed + dot_tn(kv[pair, :, hd:].reshape(2 * rows, hd), w.astype(BF16))
         return total, mixed
 
     total, mixed = loop(
-        0, n, second_pass,
+        0, lines, second_pass,
         (jnp.zeros((1, heads * rows), F32), jnp.zeros((hd, heads * rows), F32)))
     inverse = 1.0 / total
     attended = jnp.where(live_lane, mixed * inverse, 0.0).astype(BF16).astype(F32)
     delta = jnp.sum(attended * g_cols, axis=0, keepdims=True)
 
-    def third_pass(i, dq):
-        p = score[i] * inverse
-        ds = (p * (pgrad[i] - delta) * scale).astype(BF16)
+    def third_pass(p, dq):
+        pair = pl.ds(2 * p, 2)
+        probs = score[pair].reshape(2 * rows, heads * rows) * inverse
+        v_part = pgrad[pair].reshape(2 * rows, heads * rows)
+        ds = (probs * (v_part - delta) * scale).astype(BF16)
         dk = dot_nn(ds, q_hats[...])
-        dv = dot_nn(p.astype(BF16), g_rows[...])
-        dq = dq + dot_tn(kv[i, :, :hd], ds)
+        dv = dot_nn(probs.astype(BF16), g_rows[...])
+        dq = dq + dot_tn(kv[pair, :, :hd].reshape(2 * rows, hd), ds)
         return dq, dk, dv
 
+    pairs = lines // 2
+
     def other_side(step, dq):
-        j = (step + 1) % lines
-        dq, dk, dv = third_pass(2 * j + 1, dq)
-        xsend[j, :, :hd] = dk.astype(BF16)
-        xsend[j, :, hd:] = dv.astype(BF16)
-        d_side(j).start()
+        p = (step + 1) % pairs
+        dq, dk, dv = third_pass(pairs + p, dq)
+        for e in range(2):
+            j = 2 * p + e
+            xsend[j, :, :hd] = dk[e * rows:(e + 1) * rows].astype(BF16)
+            xsend[j, :, hd:] = dv[e * rows:(e + 1) * rows].astype(BF16)
+            d_side(j).start()
         return dq
 
-    def own_side(j, dq):
-        dq, dk, dv = third_pass(2 * j, dq)
+    def pass_on(j, dk, dv):
         d_side(j).wait_recv()
         zsend[j, :, :hd] = (dk + xrecv[j, :, :hd].astype(F32)).astype(BF16)
         zsend[j, :, hd:] = (dv + xrecv[j, :, hd:].astype(F32)).astype(BF16)
         d_line(j).start()
+
+    def own_side(p, dq):
+        dq, dk, dv = third_pass(p, dq)
+        pass_on(2 * p, dk[:rows], dv[:rows])
+        pass_on(2 * p + 1, dk[rows:], dv[rows:])
         return dq
 
-    dq = loop(0, lines, other_side, jnp.zeros((hd, heads * rows), F32))
-    dq = loop(1, lines, own_side, dq)
+    dq = loop(0, pairs, other_side, jnp.zeros((hd, heads * rows), F32))
+    dq = loop(1, pairs, own_side, dq)
     dq, dk, dv = third_pass(0, dq)
+    pass_on(1, dk[rows:], dv[rows:])
+    dk, dv = dk[:rows], dv[:rows]
 
     part_q = jnp.zeros((1, hd), F32)
     part_k = jnp.zeros((1, hd), F32)

time: 36.4 us -> 36.8 us (1.011)
  no operation moved by 1% of the time
where the time goes in v4:
time: 36.8 us; the launch traced here: 36.6 us
  Pallas kernels  35.3 us (96%)
  between operations  1.29 us (4%)
    pallas_call x1, Pallas kernels, per_device(): pl.pallas_call(functools.partial(kernel, n, groups), out_shape=[jax.Shape...  33.6 us
    pallas_call x1, Pallas kernels, per_device(): pl.pallas_call(store_kernel, out_shape=[jax.ShapeDtypeStruct(o.shape, o.d...  1.75 us

profile of v4, /device:TPU:0, one launch (start us, length us, event | category | flops | bytes accessed | tf_op | source)
XLA Modules:
  0.0 36.6 jit_solution(6598530682156953422)
XLA Ops:
  1.3 33.6 %shard_map.127 = (bf16[128,512]{1,0:T(8,128)(2,1)}, bf16[128,512]{1,0:T(8,128)(2,1)}, bf16[128,128]{1,0:T(8,128)(2,1)}, bf16[128,128]{1,0:T(8,128)(2,1)}, f32[1,128]{1,0:T(1,128)}, /*index=5*/f32[1,128]{1,0:T(1,128)}) custom-call(s32[16]{0:T(128)} %order_ref.1, s32[1]{0:T(128)S(6)} %copy.14.len_ref, bf16[128,512]{1,0:T(8,128)(2,1)} %bitcast.12, ...), custom_call_target="tpu_custom_call" | custom-call | tf_op jit(solution)/shard_map/pallas_call | solution.py:360
  34.8 1.7 %shard_map.128 = (bf16[128,512]{1,0:T(8,128)(2,1)}, bf16[128,512]{1,0:T(8,128)(2,1)}, bf16[128,128]{1,0:T(8,128)(2,1)}, bf16[128,128]{1,0:T(8,128)(2,1)}, f32[1,128]{1,0:T(1,128)}, /*index=5*/f32[1,128]{1,0:T(1,128)}) custom-call(bf16[128,512]{1,0:T(8,128)(2,1)} %get-tuple-element.18.refs_0_, bf16[128,512]{1,0:T(8,128)(2,1)} %get-tuple-element.19.refs_1_, ...), custom_call_target="tpu_custom_call" | custom-call | tf_op jit(solution)/shard_map/pallas_call | solution.py:408

commit v5 on v4

--- a/solution.py
+++ b/solution.py
@@ -87,12 +87,15 @@
             src_ref=src, dst_ref=dst, send_sem=send.at[i], recv_sem=recv.at[i],
             device_id={"blk": device}, device_id_type=pl.DeviceIdType.MESH)
 
-    def kv_line(j):
+    def piece(slot, part):
+        return kv.at[slot, :, pl.ds(part * hd, hd)]
+
+    def kv_line(j, part):
         device = 2 * lax.rem(line + j, lines) + side
-        return push(kv.at[0], kv.at[j], kv_send, kv_recv, j, device)
-
-    def kv_side(j):
-        return push(kv.at[j], kv.at[lines + j], kv_send, kv_recv, lines + j, partner)
+        return push(piece(0, part), piece(j, part), kv_send, kv_recv, part * n + j, device)
+
+    def kv_side(j, part):
+        return push(piece(j, part), piece(lines + j, part), kv_send, kv_recv, part * n + lines + j, partner)
 
     def d_side(j):
         return push(xsend.at[j], xrecv.at[j], x_send, x_recv, j, partner)
@@ -111,7 +114,7 @@
             src_ref=gain2.at[slot], dst_ref=gain2.at[slot], send_sem=g2_send.at[i], recv_sem=g2_recv.at[i],
             device_id={"dp": lax.rem(group + i, groups)}, device_id_type=pl.DeviceIdType.MESH)
 
-    for load in loads[:3]:
+    for load in loads[:2]:
         load.wait()
     k_gain = kg_ref[...]
     k_float = k_ref[...].astype(F32)
@@ -120,13 +123,18 @@
 
     pl.semaphore_wait(barrier, n - 1 + groups - 1)
 
-    kv_side(0).start()
-
-    def start_kv(j, _):
-        kv_line(j).start()
-        return _
-
-    loop(1, lines, start_kv, 0)
+    def start_kv(part):
+        kv_side(0, part).start()
+
+        def start_line(j, _):
+            kv_line(j, part).start()
+            return _
+
+        loop(1, lines, start_line, 0)
+
+    start_kv(0)
+    loads[2].wait()
+    start_kv(1)
     for load in loads[3:]:
         load.wait()
     q_gain = qg_ref[...]
@@ -162,20 +170,27 @@
         s = dot_nt(kv[i, :, :hd], q_hats[...]) * (scale * LOG2E)
         s = s + jnp.concatenate([bias] * heads, axis=1)
         score[i] = s
+        return jnp.maximum(top, jnp.max(s, axis=0, keepdims=True))
+
+    def value_pass(i, carry):
         pgrad[i] = dot_nt(kv[i, :, hd:], g_rows[...])
-        return jnp.maximum(top, jnp.max(s, axis=0, keepdims=True))
-
-    def first_pass_remote(j, top):
-        kv_line(j).wait_recv()
-        kv_side(j).start()
-        top = first_pass(j, top)
-        kv_side(j - 1).wait_recv()
-        return first_pass(lines + j - 1, top)
-
-    top = first_pass(0, jnp.full((1, heads * rows), MASKED, F32))
-    top = loop(1, lines, first_pass_remote, top)
-    kv_side(lines - 1).wait_recv()
-    top = first_pass(n - 1, top)
+        return carry
+
+    def arrivals(part, work, carry):
+        def step(j, carry):
+            kv_line(j, part).wait_recv()
+            kv_side(j, part).start()
+            carry = work(j, carry)
+            kv_side(j - 1, part).wait_recv()
+            return work(lines + j - 1, carry)
+
+        carry = work(0, carry)
+        carry = loop(1, lines, step, carry)
+        kv_side(lines - 1, part).wait_recv()
+        return work(n - 1, carry)
+
+    top = arrivals(0, first_pass, jnp.full((1, heads * rows), MASKED, F32))
+    arrivals(1, value_pass, 0)
 
     def second_pass(p, carry):
         total, mixed = carry
@@ -314,12 +329,14 @@
     loop(1, n, drain, 0)
 
     def drain_side(j, _):
-        kv_side(j).wait_send()
+        kv_side(j, 0).wait_send()
+        kv_side(j, 1).wait_send()
         d_side(j).wait_send()
         return _
 
     def drain_line(j, _):
-        kv_line(j).wait_send()
+        kv_line(j, 0).wait_send()
+        kv_line(j, 1).wait_send()
         d_line(j).wait_send()
         return _
 
@@ -394,7 +411,7 @@
             pltpu.VMEM((groups, 2, hd), F32),
             pltpu.VMEM((lanes, hd), BF16),
             pltpu.VMEM((lanes, hd), BF16),
-            dma((n,)), dma((n,)),
+            dma((2 * n,)), dma((2 * n,)),
             dma((n // 2,)), dma((n // 2,)), dma((n // 2,)), dma((n // 2,)),
             dma((n,)), dma((n,)), dma((groups,)), dma((groups,)),
         ],

time: 36.8 us -> 40.8 us (1.11)
  Pallas kernels: 35.3 us -> 39.3 us
    pallas_call x1, Pallas kernels: 33.6 us -> 37.6 us  [per_device(): pl.pallas_call(functools.partial(kernel, n, groups), out_shape=[jax.Shape...]
where the time goes in v5:
time: 40.8 us; the launch traced here: 40.6 us
  Pallas kernels  39.3 us (96%)
  between operations  1.29 us (3%)
    pallas_call x1, Pallas kernels, per_device(): pl.pallas_call(functools.partial(kernel, n, groups), out_shape=[jax.Shape...  37.6 us
    pallas_call x1, Pallas kernels, per_device(): pl.pallas_call(store_kernel, out_shape=[jax.ShapeDtypeStruct(o.shape, o.d...  1.75 us

profile of v5, /device:TPU:0, one launch (start us, length us, event | category | flops | bytes accessed | tf_op | source)
XLA Modules:
  0.0 40.6 jit_solution(15025161032469378150)
XLA Ops:
  1.3 37.6 %shard_map.127 = (bf16[128,512]{1,0:T(8,128)(2,1)}, bf16[128,512]{1,0:T(8,128)(2,1)}, bf16[128,128]{1,0:T(8,128)(2,1)}, bf16[128,128]{1,0:T(8,128)(2,1)}, f32[1,128]{1,0:T(1,128)}, /*index=5*/f32[1,128]{1,0:T(1,128)}) custom-call(s32[16]{0:T(128)} %order_ref.1, s32[1]{0:T(128)S(6)} %copy.14.len_ref, bf16[128,512]{1,0:T(8,128)(2,1)} %bitcast.12, ...), custom_call_target="tpu_custom_call" | custom-call | tf_op jit(solution)/shard_map/pallas_call | solution.py:377
  38.9 1.7 %shard_map.128 = (bf16[128,512]{1,0:T(8,128)(2,1)}, bf16[128,512]{1,0:T(8,128)(2,1)}, bf16[128,128]{1,0:T(8,128)(2,1)}, bf16[128,128]{1,0:T(8,128)(2,1)}, f32[1,128]{1,0:T(1,128)}, /*index=5*/f32[1,128]{1,0:T(1,128)}) custom-call(bf16[128,512]{1,0:T(8,128)(2,1)} %get-tuple-element.18.refs_0_, bf16[128,512]{1,0:T(8,128)(2,1)} %get-tuple-element.19.refs_1_, ...), custom_call_target="tpu_custom_call" | custom-call | tf_op jit(solution)/shard_map/pallas_call | solution.py:425

commit v6 on v4

--- a/solution.py
+++ b/solution.py
@@ -122,8 +122,11 @@
 
     kv_side(0).start()
 
-    def start_kv(j, _):
-        kv_line(j).start()
+    def turn(i):
+        return 1 + (i - 1 + lines // 2 - 1) % (lines - 1)
+
+    def start_kv(i, _):
+        kv_line(turn(i)).start()
         return _
 
     loop(1, lines, start_kv, 0)
@@ -165,17 +168,20 @@
         pgrad[i] = dot_nt(kv[i, :, hd:], g_rows[...])
         return jnp.maximum(top, jnp.max(s, axis=0, keepdims=True))
 
-    def first_pass_remote(j, top):
+    def first_pass_remote(i, top):
+        j = turn(i)
+        before = turn(i - 1) * ((i + lines - 2) // lines)
         kv_line(j).wait_recv()
         kv_side(j).start()
         top = first_pass(j, top)
-        kv_side(j - 1).wait_recv()
-        return first_pass(lines + j - 1, top)
+        kv_side(before).wait_recv()
+        return first_pass(lines + before, top)
 
     top = first_pass(0, jnp.full((1, heads * rows), MASKED, F32))
     top = loop(1, lines, first_pass_remote, top)
-    kv_side(lines - 1).wait_recv()
-    top = first_pass(n - 1, top)
+    last = turn(lines - 1)
+    kv_side(last).wait_recv()
+    top = first_pass(lines + last, top)
 
     def second_pass(p, carry):
         total, mixed = carry

time: 36.8 us -> 38.6 us (1.049)
  Pallas kernels: 35.3 us -> 37.1 us
    pallas_call x1, Pallas kernels: 33.6 us -> 35.4 us  [per_device(): pl.pallas_call(functools.partial(kernel, n, groups), out_shape=[jax.Shape...]
where the time goes in v6:
time: 38.6 us; the launch traced here: 38.4 us
  Pallas kernels  37.1 us (96%)
  between operations  1.29 us (3%)
    pallas_call x1, Pallas kernels, per_device(): pl.pallas_call(functools.partial(kernel, n, groups), out_shape=[jax.Shape...  35.4 us
    pallas_call x1, Pallas kernels, per_device(): pl.pallas_call(store_kernel, out_shape=[jax.ShapeDtypeStruct(o.shape, o.d...  1.75 us

profile of v6, /device:TPU:0, one launch (start us, length us, event | category | flops | bytes accessed | tf_op | source)
XLA Modules:
  0.0 38.4 jit_solution(9786563161433740595)
XLA Ops:
  1.3 35.4 %shard_map.127 = (bf16[128,512]{1,0:T(8,128)(2,1)}, bf16[128,512]{1,0:T(8,128)(2,1)}, bf16[128,128]{1,0:T(8,128)(2,1)}, bf16[128,128]{1,0:T(8,128)(2,1)}, f32[1,128]{1,0:T(1,128)}, /*index=5*/f32[1,128]{1,0:T(1,128)}) custom-call(s32[16]{0:T(128)} %order_ref.1, s32[1]{0:T(128)S(6)} %copy.14.len_ref, bf16[128,512]{1,0:T(8,128)(2,1)} %bitcast.12, ...), custom_call_target="tpu_custom_call" | custom-call | tf_op jit(solution)/shard_map/pallas_call | solution.py:366
  36.7 1.7 %shard_map.128 = (bf16[128,512]{1,0:T(8,128)(2,1)}, bf16[128,512]{1,0:T(8,128)(2,1)}, bf16[128,128]{1,0:T(8,128)(2,1)}, bf16[128,128]{1,0:T(8,128)(2,1)}, f32[1,128]{1,0:T(1,128)}, /*index=5*/f32[1,128]{1,0:T(1,128)}) custom-call(bf16[128,512]{1,0:T(8,128)(2,1)} %get-tuple-element.18.refs_0_, bf16[128,512]{1,0:T(8,128)(2,1)} %get-tuple-element.19.refs_1_, ...), custom_call_target="tpu_custom_call" | custom-call | tf_op jit(solution)/shard_map/pallas_call | solution.py:414
